TPU v7x, 32 devices: a whole 2x2x4 slice. The times are simulated.
32 devices in a mesh: fsdp: 32 (over z, y, x, core).
Axes of the slice: x: 2, y: 2, z: 4, core: 2. Of those that a mesh axis runs over, the one named last changes fastest.
Arguments:
- tokens: bfloat16 [4096, 768], P('fsdp')
- doc_ids: int32 [4096], P('fsdp'), may hold values from 0 to 3, as said below
- pad_mask: int32 [4096], P('fsdp'), may hold values from 0 to 1, as said below
- qkv_matrix: bfloat16 [768, 2304], P('fsdp'), may hold values from -0.21875 to 0.21875
- query_bias: bfloat16 [768], P('fsdp'), may hold values from -3 to 3
- value_bias: bfloat16 [768], P('fsdp'), may hold values from -3 to 3
- out_matrix: bfloat16 [768, 768], P('fsdp'), may hold values from -1.75 to 1.75
- out_bias: bfloat16 [768], P('fsdp'), may hold values from -3 to 3
- attn_gain: bfloat16 [768], P('fsdp'), may hold values from 0.25 to 1.75
- attn_shift: bfloat16 [768], P('fsdp'), may hold values from -3 to 3
- up_matrix: bfloat16 [768, 3072], P('fsdp'), may hold values from -0.21875 to 0.21875
- up_bias: bfloat16 [3072], P('fsdp'), may hold values from -3 to 3
- down_matrix: bfloat16 [3072, 768], P('fsdp'), may hold values from -0.109375 to 0.109375
- down_bias: bfloat16 [768], P('fsdp'), may hold values from -3 to 3
- ffn_gain: bfloat16 [768], P('fsdp'), may hold values from 0.25 to 1.75
- ffn_shift: bfloat16 [768], P('fsdp'), may hold values from -3 to 3
- cotangent: bfloat16 [4096, 768], P('fsdp'), may hold values from -6 to 6
Outputs:
- layer_out: bfloat16 [4096, 768], P('fsdp')
- token_grad: float32 [4096, 768], P('fsdp')
- grad_qkv: float32 [768, 2304], P('fsdp')
- grad_qbias: float32 [768], P('fsdp')
- grad_vbias: float32 [768], P('fsdp')
- grad_outmat: float32 [768, 768], P('fsdp')
- grad_outbias: float32 [768], P('fsdp')
- grad_gain_one: float32 [768], P('fsdp')
- grad_shift_one: float32 [768], P('fsdp')
- grad_upmat: float32 [768, 3072], P('fsdp')
- grad_upbias: float32 [3072], P('fsdp')
- grad_downmat: float32 [3072, 768], P('fsdp')
- grad_downbias: float32 [768], P('fsdp')
- grad_gain_two: float32 [768], P('fsdp')
- grad_shift_two: float32 [768], P('fsdp')
Inputs may be any that keep to these rules, and one draw needn't show every extreme that they name: `doc_ids`: within each block of 128 rows the ids never fall; the first row has 0 and the last 3; rows with one id are one sequence, padding continues the last one. `pad_mask`: within each block of 128 rows the ones come first and number from 32 to 128; some block is all ones and some has exactly 32.
All inputs are finite; a program needn't handle non-finite values.
Results may differ from a plain program's by a relative error of at most 0.01.
Values may be sent and summed in bfloat16 or wider, within the bound.
A program may use at most 192 MiB of HBM per device.

v0:
```python
import math

import jax
import jax.numpy as jnp
from jax import lax
from jax.sharding import PartitionSpec as P

HEADS = 12


norm_eps = 1e-06
root_half = 0.7071067811865476
inv_root_two_pi = 0.3989422804014327


def layer_norm(values, gain, shift):
    centred = values - jnp.mean(values, axis=-1, keepdims=True)
    inverse = lax.rsqrt(jnp.mean(centred * centred, axis=-1, keepdims=True) + norm_eps)
    normed = centred * inverse
    return (normed * gain + shift, normed, inverse)


def norm_back(upstream, normed, inverse, gain):
    scaled = upstream * gain
    return inverse * (
        scaled
        - jnp.mean(scaled, axis=-1, keepdims=True)
        - normed * jnp.mean(scaled * normed, axis=-1, keepdims=True)
    )


def masked_scores(query, key_rows, visible, score_scale):
    scores = (
        jnp.einsum("qhd,khd->hqk", query, key_rows, preferred_element_type=jnp.float32)
        * score_scale
    )
    return jnp.where(visible[None], scores, -1e30)


def grad_rows(left, right, count, ratio):
    product = jnp.einsum("ra,rb->ab", left, right, preferred_element_type=jnp.float32)
    return product.reshape(count, ratio * right.shape[1])


def local(
    tokens,
    doc_ids,
    pad_mask,
    qkv_matrix,
    query_bias,
    value_bias,
    out_matrix,
    out_bias,
    attn_gain,
    attn_shift,
    up_matrix,
    up_bias,
    down_matrix,
    down_bias,
    ffn_gain,
    ffn_shift,
    cotangent,
):
    fl = jnp.float32
    gathered = (
        lax.all_gather(qkv_matrix, "fsdp", axis=0, tiled=True),
        lax.all_gather(query_bias, "fsdp", axis=0, tiled=True),
        lax.all_gather(value_bias, "fsdp", axis=0, tiled=True),
        lax.all_gather(out_matrix, "fsdp", axis=0, tiled=True),
        lax.all_gather(out_bias, "fsdp", axis=0, tiled=True),
        lax.all_gather(attn_gain, "fsdp", axis=0, tiled=True),
        lax.all_gather(attn_shift, "fsdp", axis=0, tiled=True),
        lax.all_gather(up_matrix, "fsdp", axis=0, tiled=True),
        lax.all_gather(up_bias, "fsdp", axis=0, tiled=True),
        lax.all_gather(down_matrix, "fsdp", axis=0, tiled=True),
        lax.all_gather(down_bias, "fsdp", axis=0, tiled=True),
        lax.all_gather(ffn_gain, "fsdp", axis=0, tiled=True),
        lax.all_gather(ffn_shift, "fsdp", axis=0, tiled=True),
    )
    (
        qkv_full,
        qbias_full,
        vbias_full,
        outm_full,
        outb_full,
        gain_one,
        shift_one,
        upm_full,
        upb_full,
        downm_full,
        downb_full,
        gain_two,
        shift_two,
    ) = gathered
    row_count, model_width = tokens.shape
    head_size = model_width // HEADS
    score_scale = 1.0 / math.sqrt(head_size)
    hidden_width = upm_full.shape[1]
    ratio = hidden_width // model_width
    owned_rows = model_width // lax.axis_size("fsdp")
    zero_part = jnp.zeros((model_width,), fl)
    qkv = jnp.dot(tokens, qkv_full, preferred_element_type=fl)
    qkv = (qkv + jnp.concatenate([qbias_full.astype(fl), zero_part, vbias_full.astype(fl)])).astype(
        jnp.bfloat16
    )
    query = qkv[:, :model_width].reshape(row_count, HEADS, head_size)
    key_rows = qkv[:, model_width : 2 * model_width].reshape(row_count, HEADS, head_size)
    value_rows = qkv[:, 2 * model_width :].reshape(row_count, HEADS, head_size)
    positions = jnp.arange(row_count)
    visible = (doc_ids[:, None] == doc_ids[None, :]) & (
        (pad_mask[None, :] == 1) | (positions[:, None] == positions[None, :])
    )
    scores = masked_scores(query, key_rows, visible, score_scale)
    row_max = jnp.max(scores, axis=-1, keepdims=True)
    log_total = row_max + jnp.log(jnp.sum(jnp.exp(scores - row_max), axis=-1, keepdims=True))
    probs_b = jnp.exp(scores - log_total).astype(jnp.bfloat16)
    context = jnp.einsum("hqk,khd->qhd", probs_b, value_rows, preferred_element_type=fl)
    context = context.reshape(row_count, model_width).astype(jnp.bfloat16)
    attn_sum = (
        tokens.astype(fl)
        + jnp.dot(context, outm_full, preferred_element_type=fl)
        + outb_full.astype(fl)
    )
    hidden, normed_one, inverse_one = layer_norm(
        attn_sum, gain_one.astype(fl), shift_one.astype(fl)
    )
    hidden_b = hidden.astype(jnp.bfloat16)
    pre_act = jnp.dot(hidden_b, upm_full, preferred_element_type=fl) + upb_full.astype(fl)
    cdf_part = 0.5 * (1.0 + jax.scipy.special.erf(pre_act * root_half))
    pdf_part = jnp.exp(-0.5 * pre_act * pre_act) * inv_root_two_pi
    activation = (pre_act * cdf_part).astype(jnp.bfloat16)
    ffn_sum = (
        hidden + jnp.dot(activation, downm_full, preferred_element_type=fl) + downb_full.astype(fl)
    )
    normed_out, normed_two, inverse_two = layer_norm(
        ffn_sum, gain_two.astype(fl), shift_two.astype(fl)
    )
    layer_out = normed_out.astype(jnp.bfloat16)
    again = (
        lax.all_gather(qkv_matrix, "fsdp", axis=0, tiled=True),
        lax.all_gather(query_bias, "fsdp", axis=0, tiled=True),
        lax.all_gather(value_bias, "fsdp", axis=0, tiled=True),
        lax.all_gather(out_matrix, "fsdp", axis=0, tiled=True),
        lax.all_gather(out_bias, "fsdp", axis=0, tiled=True),
        lax.all_gather(attn_gain, "fsdp", axis=0, tiled=True),
        lax.all_gather(attn_shift, "fsdp", axis=0, tiled=True),
        lax.all_gather(up_matrix, "fsdp", axis=0, tiled=True),
        lax.all_gather(up_bias, "fsdp", axis=0, tiled=True),
        lax.all_gather(down_matrix, "fsdp", axis=0, tiled=True),
        lax.all_gather(down_bias, "fsdp", axis=0, tiled=True),
        lax.all_gather(ffn_gain, "fsdp", axis=0, tiled=True),
        lax.all_gather(ffn_shift, "fsdp", axis=0, tiled=True),
    )
    (
        qkv_back,
        qbias_back,
        vbias_back,
        outm_back,
        outb_back,
        gain_one_back,
        shift_one_back,
        upm_back,
        upb_back,
        downm_back,
        downb_back,
        gain_two_back,
        shift_two_back,
    ) = again
    upstream = cotangent.astype(fl)
    g_gain_two = jnp.sum(upstream * normed_two, axis=0)
    g_shift_two = jnp.sum(upstream, axis=0)
    d_ffn = norm_back(upstream, normed_two, inverse_two, gain_two_back.astype(fl))
    g_down_b = jnp.sum(d_ffn, axis=0)
    d_ffn_b = d_ffn.astype(jnp.bfloat16)
    d_act = jnp.einsum("rd,fd->rf", d_ffn_b, downm_back, preferred_element_type=fl)
    d_pre = d_act * (cdf_part + pre_act * pdf_part)
    g_up_b = jnp.sum(d_pre, axis=0)
    d_pre_b = d_pre.astype(jnp.bfloat16)
    d_hidden = d_ffn + jnp.einsum("rf,df->rd", d_pre_b, upm_back, preferred_element_type=fl)
    ffn_vectors = jnp.concatenate(
        [
            jnp.stack([g_down_b, g_gain_two, g_shift_two], axis=1),
            g_up_b.reshape(model_width, ratio),
        ],
        axis=1,
    )
    g_gain_one = jnp.sum(d_hidden * normed_one, axis=0)
    g_shift_one = jnp.sum(d_hidden, axis=0)
    d_attn = norm_back(d_hidden, normed_one, inverse_one, gain_one_back.astype(fl))
    g_out_b = jnp.sum(d_attn, axis=0)
    d_attn_b = d_attn.astype(jnp.bfloat16)
    d_context = jnp.einsum("re,de->rd", d_attn_b, outm_back, preferred_element_type=fl).astype(
        jnp.bfloat16
    )
    d_context = d_context.reshape(row_count, HEADS, head_size)
    again_scores = masked_scores(query, key_rows, visible, score_scale)
    probs_f = jnp.exp(again_scores - log_total)
    again_probs = probs_f.astype(jnp.bfloat16)
    d_value = jnp.einsum("hqk,qhd->khd", again_probs, d_context, preferred_element_type=fl)
    d_probs = jnp.einsum("qhd,khd->hqk", d_context, value_rows, preferred_element_type=fl)
    delta = jnp.sum(probs_f * d_probs, axis=-1, keepdims=True)
    d_scores = (probs_f * (d_probs - delta) * score_scale).astype(jnp.bfloat16)
    d_query = jnp.einsum("hqk,khd->qhd", d_scores, key_rows, preferred_element_type=fl).reshape(
        row_count, model_width
    )
    d_key = jnp.einsum("hqk,qhd->khd", d_scores, query, preferred_element_type=fl).reshape(
        row_count, model_width
    )
    d_value = d_value.reshape(row_count, model_width)
    g_qbias = jnp.sum(d_query, axis=0)
    g_vbias = jnp.sum(d_value, axis=0)
    d_qkv = jnp.concatenate([d_query, d_key, d_value], axis=1).astype(jnp.bfloat16)
    token_grad = d_attn + jnp.einsum("re,de->rd", d_qkv, qkv_back, preferred_element_type=fl)
    attn_vectors = jnp.stack([g_qbias, g_vbias, g_out_b, g_gain_one, g_shift_one], axis=1)
    owned_all = lax.psum_scatter(
        jnp.concatenate(
            [
                jnp.concatenate(
                    [
                        grad_rows(tokens, d_qkv, lax.axis_size("fsdp") * owned_rows, 1),
                        grad_rows(context, d_attn_b, lax.axis_size("fsdp") * owned_rows, 1),
                        attn_vectors,
                    ],
                    axis=1,
                ),
                jnp.concatenate(
                    [
                        grad_rows(hidden_b, d_pre_b, lax.axis_size("fsdp") * owned_rows, 1),
                        grad_rows(activation, d_ffn_b, lax.axis_size("fsdp") * owned_rows, ratio),
                        ffn_vectors,
                    ],
                    axis=1,
                ),
            ],
            axis=1,
        ),
        "fsdp",
        scatter_dimension=0,
        tiled=True,
    )
    attn_owned = owned_all[:, : 4 * model_width + 5]
    ffn_owned = owned_all[:, 4 * model_width + 5 :]
    local_rows = attn_owned.shape[0]
    w3 = 3 * model_width
    w4 = 4 * model_width
    grad_qkv = attn_owned[:, :w3]
    grad_outmat = attn_owned[:, w3:w4]
    grad_upmat = ffn_owned[:, :hidden_width]
    grad_downmat = ffn_owned[:, hidden_width : 2 * hidden_width].reshape(
        local_rows * ratio, model_width
    )
    tail = 2 * hidden_width
    grad_upbias = ffn_owned[:, tail + 3 : tail + 3 + ratio].reshape(local_rows * ratio)
    return (
        layer_out,
        token_grad,
        grad_qkv,
        attn_owned[:, w4],
        attn_owned[:, w4 + 1],
        grad_outmat,
        attn_owned[:, w4 + 2],
        attn_owned[:, w4 + 3],
        attn_owned[:, w4 + 4],
        grad_upmat,
        grad_upbias,
        grad_downmat,
        ffn_owned[:, tail],
        ffn_owned[:, tail + 1],
        ffn_owned[:, tail + 2],
    )


def solution(mesh):
    placed = (
        P("fsdp", None),
        P("fsdp"),
        P("fsdp"),
        P("fsdp", None),
        P("fsdp"),
        P("fsdp"),
        P("fsdp", None),
        P("fsdp"),
        P("fsdp"),
        P("fsdp"),
        P("fsdp", None),
        P("fsdp"),
        P("fsdp", None),
        P("fsdp"),
        P("fsdp"),
        P("fsdp"),
        P("fsdp", None),
    )
    return jax.shard_map(
        local,
        mesh=mesh,
        in_specs=placed,
        out_specs=(
            P("fsdp", None),
            P("fsdp", None),
            P("fsdp", None),
            P("fsdp"),
            P("fsdp"),
            P("fsdp", None),
            P("fsdp"),
            P("fsdp"),
            P("fsdp"),
            P("fsdp", None),
            P("fsdp"),
            P("fsdp", None),
            P("fsdp"),
            P("fsdp"),
            P("fsdp"),
        ),
        check_vma=False,
    )
```

profile of v0, /device:TPU:0, one launch (start us, length us, event | category | flops | bytes accessed | tf_op | source)
XLA Modules:
  0.0 814.0 jit_solution(12012894444269763715)
XLA Ops:
  7.2 0.7 all-gather.5.cloned.1.call-update
  8.0 0.7 all-gather.7.cloned.1.call-update
  8.7 0.7 all-gather.9.cloned.1.call-update
  9.4 0.5 all-gather.11.cloned.1.call-update
  10.0 0.8 dynamic-update-slice.1
  10.9 0.8 dynamic-update-slice
  11.7 0.8 dynamic-update-slice.2
  12.6 0.8 dynamic-update-slice.6
  13.4 0.8 dynamic-update-slice.4
  14.2 0.8 dynamic-update-slice.3
  15.1 0.8 dynamic-update-slice.8
  15.9 0.8 dynamic-update-slice.7
  16.7 0.8 dynamic-update-slice.5
  17.6 42.7 %all-reduce.10 = (bf16[768]{0:T(1024)(128)(2,1)S(1)}, bf16[768]{0:T(1024)(128)(2,1)S(1)}, bf16[768]{0:T(1024)(128)(2,1)S(1)}, bf16[768]{0:T(1024)(128)(2,1)S(1)}...) all-reduce(bf16[768]{0:T(1024)(128)(2,1)S(1)} %dynamic-update-slice, ...), channel_id=1, replica_groups=mesh['fsdp'=32] {'fsdp'}, use_global_device_ids=true, to_apply=%add.1 | all-reduce | flops 9216 | bytes 36864
  60.5 0.7 broadcast_compare_fusion
  61.1 0.8 fusion.44
  62.0 11.9 %all-gather.5.cloned.1.call-done = bf16[768,2304]{1,0:T(8,128)(2,1)} async-done(((bf16[24,2304]{1,0:T(8,128)(2,1)}), bf16[768,2304]{1,0:T(8,128)(2,1)}) %all-gather.5.cloned.1.call-update) | async-done | bytes 3538960 | tf_op jit(solution)/shard_map/all_gather | solution.py:66
  73.9 2.8 fusion.1
  77.3 0.3 fusion.60
  77.8 0.2 convolution_convert_fusion.2
  78.0 51.8 %all-gather.7.cloned.1.call-done = bf16[768,768]{1,0:T(8,128)(2,1)} async-done(((bf16[24,768]{1,0:T(8,128)(2,1)}), bf16[768,768]{1,0:T(8,128)(2,1)}) %all-gather.7.cloned.1.call-update) | async-done | bytes 1179664 | tf_op jit(solution)/shard_map/all_gather | solution.py:69
  129.8 1.7 fusion.61
  131.6 0.2 multiply_reduce_fusion.4
  131.8 63.5 %all-gather.9.cloned.1.call-done = bf16[768,3072]{1,0:T(8,128)(2,1)} async-done(((bf16[24,3072]{1,0:T(8,128)(2,1)}), bf16[768,3072]{1,0:T(8,128)(2,1)}) %all-gather.9.cloned.1.call-update) | async-done | bytes 4718608 | tf_op jit(solution)/shard_map/all_gather | solution.py:73
  195.3 3.2 convolution_add_fusion.1
  198.5 62.0 %all-gather.11.cloned.1.call-done = bf16[3072,768]{1,0:T(8,128)(2,1)} async-done(((bf16[96,768]{1,0:T(8,128)(2,1)}), bf16[3072,768]{1,0:T(8,128)(2,1)}) %all-gather.11.cloned.1.call-update) | async-done | bytes 4718608 | tf_op jit(solution)/shard_map/all_gather | solution.py:75
  260.6 3.5 fusion.62
  264.0 0.2 multiply_reduce_fusion.3
  264.3 0.8 fusion.24
  265.0 1.5 fusion.53
  266.5 2.3 fusion.65
  268.9 2.3 multiply_reduce_fusion.1
  271.2 1.5 fusion.55
  272.7 1.2 convolution_convert_fusion.1
  274.0 1.7 copy.68
  275.7 2.6 fusion.58
  278.3 2.2 fusion.66
  280.5 2.5 convolution_convert_fusion
  283.0 3.1 fusion.59
  286.1 2.8 fusion.37
  289.0 5.2 fusion.25
  294.2 5.1 fusion.40
  299.3 4.1 convolution_bitcast_fusion
  303.4 8.1 copy.72
  311.5 0.3 stack.32
  311.8 0.3 stack.33
  312.3 0.9 stack.35
  313.3 0.9 stack.36
  314.2 11.6 %reshape.194 = f32[768,3072]{1,0:T(8,128)} reshape(f32[3072,768]{1,0:T(8,128)} %fusion.40) | data formatting | bytes 18874368 | tf_op jit(solution)/shard_map/reshape | solution.py:42
  325.8 0.9 stack.37
  326.7 0.9 stack.38
  327.6 0.9 stack.39
  328.5 1.8 reshape.195
  330.4 34.6 %concatenate.12 = f32[768,9228]{1,0:T(8,128)} concatenate(f32[768,2304]{1,0:T(8,128)} %copy.72, f32[768,768]{1,0:T(8,128)S(1)} %copy-done.1, f32[768,1]{1,0:T(8,128)S(1)} %stack.32, f32[768,1]{1,0:T(8,128)S(1)} %stack.33, f32[768,1]{1,0:T(8,128)S(1)} %stack.34, f32[768,1]{1,0:T(8,128)} %stack.35, f32[768,1]{1,0:T(8,128)} %stack.36, f32[768,3072]{1,0:T(8,128)} %fusion.25, ...), dimensions={1} | concatenate | bytes 56696832 | tf_op jit(solution)/shard_map/concatenate | solution.py:216
  365.0 2.0 copy-done
  366.9 3.3 convolution_add_fusion.3
  370.3 427.9 %all-reduce.13.cloned.1.call-done = f32[768,9228]{1,0:T(8,128)} async-done(((f32[768,9228]{1,0:T(8,128)}), f32[768,9228]{1,0:T(8,128)}) %all-reduce.13.cloned.1.call-update) | async-done | bytes 28348432
  798.2 0.8 dynamic-slice.9
  799.0 0.6 reshape.196
  799.6 2.0 fusion.56
  801.6 0.8 reshape.197
  802.4 1.6 constant_dynamic-slice_fusion
  804.0 1.6 dynamic-slice.4
  805.6 1.8 dynamic-slice_reduce_fusion
  (102 shorter events, 1.3 us)
Async XLA Ops:
  7.2 66.7 %all-gather.5.cloned.1.call-start = ((), (), s32[]{:S(2)}) async-start(), calls=%async_computation | async-start | bytes 3649536 | tf_op jit(solution)/shard_map/all_gather | solution.py:66
  7.9 121.9 %all-gather.7.cloned.1.call-start = ((), (), s32[]{:S(2)}) async-start(), calls=%async_computation.1 | async-start | bytes 1216512 | tf_op jit(solution)/shard_map/all_gather | solution.py:69
  8.7 186.6 %all-gather.9.cloned.1.call-start = ((), (), s32[]{:S(2)}) async-start(), calls=%async_computation.2 | async-start | bytes 4866048 | tf_op jit(solution)/shard_map/all_gather | solution.py:73
  9.4 251.2 %all-gather.11.cloned.1.call-start = ((), (), s32[]{:S(2)}) async-start(), calls=%async_computation.3 | async-start | bytes 4866048 | tf_op jit(solution)/shard_map/all_gather | solution.py:75
  10.0 788.2 %all-reduce.13.cloned.1.call-start = ((), (), s32[]{:S(2)}) async-start(), calls=%async_computation.4 | async-start | bytes 57409536
  76.9 1.1 copy-start.10
  77.1 0.7 copy-start.15
  77.2 0.8 copy-start.14
  77.2 52.6 %copy-start.7 = (bf16[128,768]{1,0:T(8,128)(2,1)S(1)}, bf16[128,768]{1,0:T(8,128)(2,1)}, u32[]{:S(2)}) copy-start(bf16[128,768]{1,0:T(8,128)(2,1)} %param.17) | copy-start | bytes 589828
  78.0 53.8 %copy-start.11 = (bf16[12,64,128]{2,1,0:T(8,128)(2,1)}, bf16[12,64,128]{2,1,0:T(8,128)(2,1)S(1)}, u32[]{:S(2)}) copy-start(bf16[12,64,128]{2,1,0:T(8,128)(2,1)S(1)} %convolution_convert_fusion.2) | copy-start | bytes 589828
  131.6 137.3 %copy-start.18 = (f32[128]{0:T(128)}, f32[128]{0:T(128)S(1)}, u32[]{:S(2)}) copy-start(f32[128]{0:T(128)S(1)} %broadcast_multiply_fusion.5) | copy-start | bytes 1540
  131.8 137.0 %copy-start.20 = (f32[128]{0:T(128)}, f32[128]{0:T(128)S(1)}, u32[]{:S(2)}) copy-start(f32[128]{0:T(128)S(1)} %add_rsqrt_fusion.1) | copy-start | bytes 1540
  198.5 65.7 %copy-start.16 = (bf16[128,768]{1,0:T(8,128)(2,1)S(1)}, bf16[128,768]{1,0:T(8,128)(2,1)}, u32[]{:S(2)}) copy-start(bf16[128,768]{1,0:T(8,128)(2,1)} %param.33) | copy-start | bytes 589828
  260.6 5.9 copy-start.3
  265.0 3.8 slice-start
  266.5 2.3 slice-start.1
  268.8 2.4 copy-start.5
  271.2 1.5 copy-start.4
  272.7 13.4 %copy-start.2 = (f32[128,768]{1,0:T(8,128)}, f32[128,768]{1,0:T(8,128)S(1)}, u32[]{:S(2)}) copy-start(f32[128,768]{1,0:T(8,128)S(1)} %get-tuple-element.43) | copy-start | bytes 1179652
  286.1 2.9 copy-start.6
  286.1 2.9 copy-start.19
  286.1 2.9 copy-start.21
  294.2 5.1 copy-start.8
  294.2 5.1 copy-start.9
  294.2 5.1 copy-start.12
  294.2 5.1 copy-start.13
  303.4 8.1 copy-start.28
  303.4 8.4 %copy-start.17 = (f32[12,64]{1,0:T(8,128)S(1)}, f32[12,64]{1,0:T(8,128)}, u32[]{:S(2)}) copy-start(f32[12,64]{1,0:T(8,128)} %get-tuple-element.50) | copy-start | bytes 9220
  303.4 8.8 %copy-start.25 = (f32[768]{0:T(1024)S(1)}, f32[768]{0:T(1024)}, u32[]{:S(2)}) copy-start(f32[768]{0:T(1024)} %get-tuple-element.42) | copy-start | bytes 9220
  303.4 9.0 %copy-start.27 = (f32[768]{0:T(1024)S(1)}, f32[768]{0:T(1024)}, u32[]{:S(2)}) copy-start(f32[768]{0:T(1024)} %get-tuple-element.23) | copy-start | bytes 9220
  311.5 1.8 copy-start.26
  314.2 11.6 %copy-start.24 = (f32[768]{0:T(1024)S(1)}, f32[768]{0:T(1024)}, u32[]{:S(2)}) copy-start(f32[768]{0:T(1024)} %get-tuple-element.40) | copy-start | bytes 9220
  314.2 12.5 %copy-start.23 = (f32[768]{0:T(1024)S(1)}, f32[768]{0:T(1024)}, u32[]{:S(2)}) copy-start(f32[768]{0:T(1024)} %get-tuple-element.25) | copy-start | bytes 9220
  314.2 13.4 %copy-start.22 = (f32[768]{0:T(1024)S(1)}, f32[768]{0:T(1024)}, u32[]{:S(2)}) copy-start(f32[768]{0:T(1024)} %get-tuple-element.30) | copy-start | bytes 9220
  314.2 16.2 %copy-start.1 = (f32[768,768]{1,0:T(8,128)S(1)}, f32[768,768]{1,0:T(8,128)}, u32[]{:S(2)}) copy-start(f32[768,768]{1,0:T(8,128)} %fusion.37) | copy-start | bytes 7077892
  364.9 2.0 copy-start
Sparse Core Ops, SparseCore 0:
  10.9 62.9 all-gather.4
  76.8 52.9 all-gather.6
  132.7 62.5 all-gather.8
  198.1 62.4 all-gather.10
  365.1 433.0 all-reduce.12
where the time goes:
time: 816 us; the launch traced here: 814 us
  waiting for transfers between devices  620 us (76%)
  local copies, waits for them, and re-layouts  82.6 us (10%)
  matrix products  48.5 us (6%)
  blocking collectives  42.7 us (5%)
  between operations  14.2 us (2%)
    unnamed x6, waiting for transfers between devices  431 us
    all_gather x1, waiting for transfers between devices, local(): lax.all_gather(up_matrix, 'fsdp', axis=0, tiled=True)  63.5 us
    all_gather x1, waiting for transfers between devices, local(): lax.all_gather(down_matrix, 'fsdp', axis=0, tiled=True)  62 us
    all_gather x1, waiting for transfers between devices, local(): lax.all_gather(out_matrix, 'fsdp', axis=0, tiled=True)  51.8 us
    unnamed x1, blocking collectives  42.7 us
    concatenate x1, local copies, waits for them, and re-layouts, local(): jnp.concatenate([jnp.concatenate([grad_rows(tokens, d_qkv, lax.axis_size(...  34.6 us
    dot_general x4, matrix products, grad_rows(): jnp.einsum('ra,rb->ab', left, right, preferred_element_type=jnp.float32)  17.2 us
  transfers between devices with their start and end apart: 5, of which 5 were waited for; matrix products, arithmetic and copies ran while one was open for 3% of the time, Pallas kernels for 0%

commit v1 on v0

v1 whole, which is shorter than its diff:
```python
import functools
import math

import jax
import jax.numpy as jnp
from jax import lax
from jax.experimental import pallas as pl
from jax.experimental.pallas import tpu as pltpu
from jax.sharding import PartitionSpec as P

HEADS = 12
AXIS = "fsdp"
MESH_IDS = pl.DeviceIdType.MESH
BITS = 5
GROUP = 32
CORE, X, Y, Z1, Z2 = 0, 1, 2, 3, 4
SCATTER_ORDERS = (
    (CORE, X, Y, Z2, Z1),
    (CORE, X, Y, Z2, Z1),
    (CORE, Y, X, Z2, Z1),
    (CORE, Z1, Z2, X, Y),
    (CORE, Z1, Z2, X, Y),
)
VMEM_BYTES = 60 * 1024 * 1024


def bits_of(me):
    return [lax.rem(lax.div(me, 1 << b), 2) for b in range(BITS)]


def toggled(me, mine, r):
    for b in range(BITS):
        if r >> b & 1:
            me = me + (1 << b) * (1 - 2 * mine[b])
    return me


def greet(me, mine):
    barrier = pltpu.get_barrier_semaphore()
    for b in range(BITS):
        pl.semaphore_signal(
            barrier, inc=1, device_id=(toggled(me, mine, 1 << b),), device_id_type=MESH_IDS
        )
    pl.semaphore_wait(barrier, BITS)


def gather_kernel(count, *refs):
    shards, wholes = refs[:count], refs[count : 2 * count]
    send_sem, recv_sem, local_sem = refs[2 * count :]
    me = lax.axis_index(AXIS)
    mine = bits_of(me)
    greet(me, mine)

    def move(k, r, b):
        owner = toggled(me, mine, r)
        source = shards[k] if r == 0 else wholes[k].at[owner]
        slot = r | (1 << b)
        return pltpu.make_async_remote_copy(
            src_ref=source,
            dst_ref=wholes[k].at[owner],
            send_sem=send_sem.at[k, slot],
            recv_sem=recv_sem.at[k, slot],
            device_id=(toggled(me, mine, 1 << b),),
            device_id_type=MESH_IDS,
        )

    def landed(k, r):
        here = wholes[k].at[toggled(me, mine, r)]
        pltpu.make_async_remote_copy(
            src_ref=here,
            dst_ref=here,
            send_sem=send_sem.at[k, r],
            recv_sem=recv_sem.at[k, r],
            device_id=(toggled(me, mine, 1),),
            device_id_type=MESH_IDS,
        ).wait_recv()

    orders = [tuple(reversed(SCATTER_ORDERS[k])) for k in range(count)]
    own = [
        pltpu.make_async_copy(shards[k], wholes[k].at[me], local_sem.at[k]) for k in range(count)
    ]
    sent = [[] for _ in range(count)]
    for k in range(count):
        for b in orders[k]:
            copy = move(k, 0, b)
            copy.start()
            sent[k].append(copy)
    for copy in own:
        copy.start()
    have = [[0] for _ in range(count)]
    for step in range(BITS):
        width = 1 << step
        for i in range(width):
            for k in range(count):
                b = orders[k][step]
                r = have[k][i] | (1 << b)
                landed(k, r)
                for later in orders[k][step + 1 :]:
                    copy = move(k, r, later)
                    copy.start()
                    sent[k].append(copy)
        for k in range(count):
            b = orders[k][step]
            have[k] = have[k] + [r | (1 << b) for r in have[k]]
    for k in range(count):
        own[k].wait()
        for copy in sent[k]:
            copy.wait_send()


def gather_all(shards):
    count = len(shards)
    return pl.pallas_call(
        functools.partial(gather_kernel, count),
        out_shape=[jax.ShapeDtypeStruct((GROUP,) + s.shape, s.dtype) for s in shards],
        in_specs=[pl.BlockSpec(memory_space=pl.ANY)] * count,
        out_specs=[pl.BlockSpec(memory_space=pl.ANY)] * count,
        scratch_shapes=[
            pltpu.SemaphoreType.DMA((count, GROUP)),
            pltpu.SemaphoreType.DMA((count, GROUP)),
            pltpu.SemaphoreType.DMA((count,)),
        ],
        compiler_params=pltpu.CompilerParams(collective_id=0, has_side_effects=True),
        name="gather_all",
    )(*shards)


def priority(order, step):
    left = order[step + 1 :]
    blocks = [0]
    for b in reversed(left):
        blocks = [r | (1 << b) for r in blocks] + blocks
    return blocks


def scatter_kernel(count, *refs):
    parts, outs = refs[:count], refs[count : 2 * count]
    landing = refs[2 * count : 3 * count]
    send_sem, recv_sem = refs[3 * count :]
    me = lax.axis_index(AXIS)
    mine = bits_of(me)
    greet(me, mine)

    slot_of = []
    for k in range(count):
        table, used = {}, 0
        for step in range(BITS):
            for r in priority(SCATTER_ORDERS[k], step):
                table[step, r] = used
                used += 1
        slot_of.append(table)

    def held(k, step, r):
        if step < 0:
            return parts[k].at[toggled(me, mine, r)]
        return landing[k].at[slot_of[k][step, r]]

    def move(k, step, r):
        b = SCATTER_ORDERS[k][step]
        slot = slot_of[k][step, r & ~(1 << b)]
        return pltpu.make_async_remote_copy(
            src_ref=held(k, step - 1, r),
            dst_ref=landing[k].at[slot],
            send_sem=send_sem.at[k, slot],
            recv_sem=recv_sem.at[k, slot],
            device_id=(toggled(me, mine, 1 << b),),
            device_id_type=MESH_IDS,
        )

    copies = {}
    for i in range(GROUP // 2):
        for k in range(count):
            order = SCATTER_ORDERS[k]
            r = priority(order, 0)[i]
            copy = move(k, 0, r | (1 << order[0]))
            copy.start()
            copies[k, 0, r] = copy
    for step in range(BITS):
        for i in range(1 << (BITS - 1 - step)):
            for k in range(count):
                order = SCATTER_ORDERS[k]
                r = priority(order, step)[i]
                copies[k, step, r].wait_recv()
                before, now = held(k, step - 1, r), held(k, step, r)
                columns = now.shape[-1]
                last = step == BITS - 1
                tile = min(columns, 768 if now.shape[0] <= 24 else 256)

                def add(j, carry, before=before, now=now, tile=tile, last=last, k=k):
                    at = pl.ds(pl.multiple_of(j * tile, tile), tile)
                    total = now[:, at].astype(jnp.float32) + before[:, at].astype(jnp.float32)
                    if last:
                        outs[k][:, at] = total
                    else:
                        now[:, at] = total.astype(jnp.bfloat16)
                    return carry

                lax.fori_loop(0, columns // tile, add, 0)
                if not last and r >> order[step + 1] & 1:
                    copy = move(k, step + 1, r)
                    copy.start()
                    copies[k, step + 1, r & ~(1 << order[step + 1])] = copy
    for copy in copies.values():
        copy.wait_send()


def scatter_all(parts):
    count = len(parts)
    return pl.pallas_call(
        functools.partial(scatter_kernel, count),
        out_shape=[jax.ShapeDtypeStruct(p.shape[1:], jnp.float32) for p in parts],
        in_specs=[pl.BlockSpec(memory_space=pltpu.VMEM)] * count,
        out_specs=[pl.BlockSpec(memory_space=pltpu.VMEM)] * count,
        scratch_shapes=[pltpu.VMEM((GROUP - 1,) + p.shape[1:], p.dtype) for p in parts]
        + [
            pltpu.SemaphoreType.DMA((count, GROUP)),
            pltpu.SemaphoreType.DMA((count, GROUP)),
        ],
        compiler_params=pltpu.CompilerParams(
            collective_id=1, has_side_effects=True, vmem_limit_bytes=VMEM_BYTES
        ),
        name="scatter_all",
    )(*parts)


norm_eps = 1e-06
root_half = 0.7071067811865476
inv_root_two_pi = 0.3989422804014327


def layer_norm(values, gain, shift):
    centred = values - jnp.mean(values, axis=-1, keepdims=True)
    inverse = lax.rsqrt(jnp.mean(centred * centred, axis=-1, keepdims=True) + norm_eps)
    normed = centred * inverse
    return (normed * gain + shift, normed, inverse)


def norm_back(upstream, normed, inverse, gain):
    scaled = upstream * gain
    return inverse * (
        scaled
        - jnp.mean(scaled, axis=-1, keepdims=True)
        - normed * jnp.mean(scaled * normed, axis=-1, keepdims=True)
    )


def masked_scores(query, key_rows, visible, score_scale):
    scores = (
        jnp.einsum("qhd,khd->hqk", query, key_rows, preferred_element_type=jnp.float32)
        * score_scale
    )
    return jnp.where(visible[None], scores, -1e30)


def grad_rows(left, right):
    return jnp.einsum("ra,rb->ab", left, right, preferred_element_type=jnp.float32)


def local(
    tokens,
    doc_ids,
    pad_mask,
    qkv_matrix,
    query_bias,
    value_bias,
    out_matrix,
    out_bias,
    attn_gain,
    attn_shift,
    up_matrix,
    up_bias,
    down_matrix,
    down_bias,
    ffn_gain,
    ffn_shift,
    cotangent,
):
    fl = jnp.float32
    in_kernels = lax.axis_size(AXIS) == GROUP
    vectors = jnp.concatenate(
        [
            jnp.stack(
                [
                    query_bias,
                    value_bias,
                    out_bias,
                    attn_gain,
                    attn_shift,
                    down_bias,
                    ffn_gain,
                    ffn_shift,
                ],
                axis=1,
            ),
            up_bias.reshape(query_bias.shape[0], -1),
        ],
        axis=1,
    )
    vector_count = vectors.shape[1]
    if in_kernels:
        vectors = jnp.pad(vectors, ((0, 0), (0, 128 - vector_count)))
        wholes = gather_all([qkv_matrix, out_matrix, up_matrix, down_matrix, vectors])
        wholes = [w.reshape((-1, w.shape[-1])) for w in wholes]
    else:
        wholes = [
            lax.all_gather(w, AXIS, axis=0, tiled=True)
            for w in (qkv_matrix, out_matrix, up_matrix, down_matrix, vectors)
        ]
    qkv_full, outm_full, upm_full, downm_full, vectors_full = wholes
    qbias_full, vbias_full, outb_full, gain_one, shift_one, downb_full, gain_two, shift_two = (
        vectors_full[:, j] for j in range(8)
    )
    upb_full = vectors_full[:, 8:vector_count].reshape(-1)
    qkv_back, outm_back, upm_back, downm_back = qkv_full, outm_full, upm_full, downm_full
    gain_one_back, gain_two_back = gain_one, gain_two
    row_count, model_width = tokens.shape
    head_size = model_width // HEADS
    score_scale = 1.0 / math.sqrt(head_size)
    hidden_width = upm_full.shape[1]
    ratio = hidden_width // model_width
    zero_part = jnp.zeros((model_width,), fl)
    qkv = jnp.dot(tokens, qkv_full, preferred_element_type=fl)
    qkv = (qkv + jnp.concatenate([qbias_full.astype(fl), zero_part, vbias_full.astype(fl)])).astype(
        jnp.bfloat16
    )
    query = qkv[:, :model_width].reshape(row_count, HEADS, head_size)
    key_rows = qkv[:, model_width : 2 * model_width].reshape(row_count, HEADS, head_size)
    value_rows = qkv[:, 2 * model_width :].reshape(row_count, HEADS, head_size)
    positions = jnp.arange(row_count)
    visible = (doc_ids[:, None] == doc_ids[None, :]) & (
        (pad_mask[None, :] == 1) | (positions[:, None] == positions[None, :])
    )
    scores = masked_scores(query, key_rows, visible, score_scale)
    row_max = jnp.max(scores, axis=-1, keepdims=True)
    log_total = row_max + jnp.log(jnp.sum(jnp.exp(scores - row_max), axis=-1, keepdims=True))
    probs_b = jnp.exp(scores - log_total).astype(jnp.bfloat16)
    context = jnp.einsum("hqk,khd->qhd", probs_b, value_rows, preferred_element_type=fl)
    context = context.reshape(row_count, model_width).astype(jnp.bfloat16)
    attn_sum = (
        tokens.astype(fl)
        + jnp.dot(context, outm_full, preferred_element_type=fl)
        + outb_full.astype(fl)
    )
    hidden, normed_one, inverse_one = layer_norm(
        attn_sum, gain_one.astype(fl), shift_one.astype(fl)
    )
    hidden_b = hidden.astype(jnp.bfloat16)
    pre_act = jnp.dot(hidden_b, upm_full, preferred_element_type=fl) + upb_full.astype(fl)
    cdf_part = 0.5 * (1.0 + jax.scipy.special.erf(pre_act * root_half))
    pdf_part = jnp.exp(-0.5 * pre_act * pre_act) * inv_root_two_pi
    activation = (pre_act * cdf_part).astype(jnp.bfloat16)
    ffn_sum = (
        hidden + jnp.dot(activation, downm_full, preferred_element_type=fl) + downb_full.astype(fl)
    )
    normed_out, normed_two, inverse_two = layer_norm(
        ffn_sum, gain_two.astype(fl), shift_two.astype(fl)
    )
    layer_out = normed_out.astype(jnp.bfloat16)
    upstream = cotangent.astype(fl)
    g_gain_two = jnp.sum(upstream * normed_two, axis=0)
    g_shift_two = jnp.sum(upstream, axis=0)
    d_ffn = norm_back(upstream, normed_two, inverse_two, gain_two_back.astype(fl))
    g_down_b = jnp.sum(d_ffn, axis=0)
    d_ffn_b = d_ffn.astype(jnp.bfloat16)
    d_act = jnp.einsum("rd,fd->rf", d_ffn_b, downm_back, preferred_element_type=fl)
    d_pre = d_act * (cdf_part + pre_act * pdf_part)
    g_up_b = jnp.sum(d_pre, axis=0)
    d_pre_b = d_pre.astype(jnp.bfloat16)
    d_hidden = d_ffn + jnp.einsum("rf,df->rd", d_pre_b, upm_back, preferred_element_type=fl)
    g_gain_one = jnp.sum(d_hidden * normed_one, axis=0)
    g_shift_one = jnp.sum(d_hidden, axis=0)
    d_attn = norm_back(d_hidden, normed_one, inverse_one, gain_one_back.astype(fl))
    g_out_b = jnp.sum(d_attn, axis=0)
    d_attn_b = d_attn.astype(jnp.bfloat16)
    d_context = jnp.einsum("re,de->rd", d_attn_b, outm_back, preferred_element_type=fl).astype(
        jnp.bfloat16
    )
    d_context = d_context.reshape(row_count, HEADS, head_size)
    again_scores = masked_scores(query, key_rows, visible, score_scale)
    probs_f = jnp.exp(again_scores - log_total)
    again_probs = probs_f.astype(jnp.bfloat16)
    d_value = jnp.einsum("hqk,qhd->khd", again_probs, d_context, preferred_element_type=fl)
    d_probs = jnp.einsum("qhd,khd->hqk", d_context, value_rows, preferred_element_type=fl)
    delta = jnp.sum(probs_f * d_probs, axis=-1, keepdims=True)
    d_scores = (probs_f * (d_probs - delta) * score_scale).astype(jnp.bfloat16)
    d_query = jnp.einsum("hqk,khd->qhd", d_scores, key_rows, preferred_element_type=fl).reshape(
        row_count, model_width
    )
    d_key = jnp.einsum("hqk,qhd->khd", d_scores, query, preferred_element_type=fl).reshape(
        row_count, model_width
    )
    d_value = d_value.reshape(row_count, model_width)
    g_qbias = jnp.sum(d_query, axis=0)
    g_vbias = jnp.sum(d_value, axis=0)
    d_qkv = jnp.concatenate([d_query, d_key, d_value], axis=1).astype(jnp.bfloat16)
    token_grad = d_attn + jnp.einsum("re,de->rd", d_qkv, qkv_back, preferred_element_type=fl)
    sums = jnp.concatenate(
        [
            jnp.stack(
                [
                    g_qbias,
                    g_vbias,
                    g_out_b,
                    g_gain_one,
                    g_shift_one,
                    g_down_b,
                    g_gain_two,
                    g_shift_two,
                ],
                axis=1,
            ),
            g_up_b.reshape(model_width, ratio),
        ],
        axis=1,
    )
    pairs = ((tokens, d_qkv), (context, d_attn_b), (hidden_b, d_pre_b), (activation, d_ffn_b))
    if in_kernels:
        parts = [grad_rows(left, right).astype(jnp.bfloat16) for left, right in pairs]
        parts.append(jnp.pad(sums, ((0, 0), (0, 128 - vector_count))).astype(jnp.bfloat16))
        owned = scatter_all([p.reshape((GROUP, -1, p.shape[1])) for p in parts])
    else:
        owned = [
            lax.psum_scatter(p, AXIS, scatter_dimension=0, tiled=True)
            for p in [grad_rows(left, right) for left, right in pairs] + [sums]
        ]
    grad_qkv, grad_outmat, grad_upmat, grad_downmat, vec = owned
    grad_upbias = vec[:, 8:vector_count].reshape(-1)
    return (
        layer_out,
        token_grad,
        grad_qkv,
        vec[:, 0],
        vec[:, 1],
        grad_outmat,
        vec[:, 2],
        vec[:, 3],
        vec[:, 4],
        grad_upmat,
        grad_upbias,
        grad_downmat,
        vec[:, 5],
        vec[:, 6],
        vec[:, 7],
    )


def solution(mesh):
    placed = (
        P("fsdp", None),
        P("fsdp"),
        P("fsdp"),
        P("fsdp", None),
        P("fsdp"),
        P("fsdp"),
        P("fsdp", None),
        P("fsdp"),
        P("fsdp"),
        P("fsdp"),
        P("fsdp", None),
        P("fsdp"),
        P("fsdp", None),
        P("fsdp"),
        P("fsdp"),
        P("fsdp"),
        P("fsdp", None),
    )
    return jax.shard_map(
        local,
        mesh=mesh,
        in_specs=placed,
        out_specs=(
            P("fsdp", None),
            P("fsdp", None),
            P("fsdp", None),
            P("fsdp"),
            P("fsdp"),
            P("fsdp", None),
            P("fsdp"),
            P("fsdp"),
            P("fsdp"),
            P("fsdp", None),
            P("fsdp"),
            P("fsdp", None),
            P("fsdp"),
            P("fsdp"),
            P("fsdp"),
        ),
        check_vma=False,
    )
```

time: 816 us -> 230 us (0.28)
  waiting for transfers between devices: 620 us -> 0 us
  Pallas kernels: 0 us -> 150 us
  local copies, waits for them, and re-layouts: 82.6 us -> 26.6 us
  blocking collectives: 42.7 us -> 0 us
  between operations: 14.2 us -> 1.3 us
    unnamed x6 -> x0, waiting for transfers between devices: 431 us -> none
    all_gather x4 -> x0, waiting for transfers between devices: 189 us -> none  [the longest x1 63.5 us: local(): lax.all_gather(up_matrix, 'fsdp', axis=0, tiled=True)]
    pallas_call x0 -> x2, Pallas kernels: none -> 150 us  [the longest x1 80.7 us: scatter_all(): pl.pallas_call(functools.partial(scatter_kernel, count), out_shape=[jax.S...]
    unnamed x1 -> x0, blocking collectives: 42.7 us -> none
    concatenate x1 -> x2, local copies, waits for them, and re-layouts: 34.6 us -> 0.2 us  [the longest x1 0.11 us: local(): jnp.concatenate([jnp.stack([query_bias, value_bias, out_bias, attn_gain,...]
    reshape x3 -> x2, local copies, waits for them, and re-layouts: 13 us -> 1.36 us  [the longest x1 0.75 us: local(): up_bias.reshape(query_bias.shape[0], -1)]
  transfers between devices with their start and end apart: 5 -> 0, of which waited for: 5 -> 0; matrix products, arithmetic and copies ran while one was open for 3% -> 0% of each run, Pallas kernels for 0% -> 0%
where the time goes in v1:
time: 230 us; the launch traced here: 229 us
  Pallas kernels  150 us (65%)
  matrix products  41.7 us (18%)
  local copies, waits for them, and re-layouts  26.6 us (12%)
  other arithmetic  9.61 us (4%)
    pallas_call x1, Pallas kernels, scatter_all(): pl.pallas_call(functools.partial(scatter_kernel, count), out_shape=[jax.S...  80.7 us
    pallas_call x1, Pallas kernels, gather_all(): pl.pallas_call(functools.partial(gather_kernel, count), out_shape=[jax.Sh...  69.5 us
    dot_general x4, matrix products, grad_rows(): jnp.einsum('ra,rb->ab', left, right, preferred_element_type=jnp.float32)  11.7 us
    unnamed x92, local copies, waits for them, and re-layouts  10.3 us
    another operation x8, local copies, waits for them, and re-layouts, local(): jnp.stack([query_bias, value_bias, out_bias, attn_gain, attn_shift, down_...  5.97 us
    dot_general x1, matrix products, local(): jnp.einsum('rd,fd->rf', d_ffn_b, downm_back, preferred_element_type=fl)  4.72 us

profile of v1, /device:TPU:0, one launch (start us, length us, event | category | flops | bytes accessed | tf_op | source)
XLA Modules:
  0.0 229.5 jit_solution(3263437107859524242)
XLA Ops:
  0.6 0.7 copy.70
  1.4 0.7 copy.71
  2.1 0.7 copy.72
  2.9 0.7 copy.73
  3.6 0.7 copy.74
  4.4 0.7 copy.75
  5.1 0.7 copy.76
  5.9 0.7 copy.77
  6.6 0.7 reshape.263
  7.4 0.1 concatenate.14
  7.5 0.6 pad.9.refs_4_
  8.1 69.5 %gather_all.1 = (bf16[32,24,2304]{2,1,0:T(8,128)(2,1)}, bf16[32,24,768]{2,1,0:T(8,128)(2,1)}, bf16[32,24,3072]{2,1,0:T(8,128)(2,1)}, bf16[32,96,768]{2,1,0:T(8,128)(2,1)}, bf16[32,24,128]{2,1,0:T(8,128)(2,1)}) custom-call(bf16[24,2304]{1,0:T(8,128)(2,1)} %refs_0_.1, bf16[24,768]{1,0:T(8,128)(2,1)} %refs_1_.1, bf16[24,3072]{1,0:T(8,128)(2,1)} %refs_2_.1, ...), custom_call_target="tpu_custom_call" | custom-call | tf_op jit(solution)/shard_map/gather_all/pallas_call | solution.py:113
  77.7 2.1 fusion.57
  79.7 0.1 copy.92
  79.8 0.6 convert_reduce_fusion.7
  80.5 1.0 slice_convert_fusion
  81.5 0.2 reshape.288
  81.8 0.6 convert_reduce_fusion.1
  82.4 3.7 %fusion.2 = bf16[128,2304]{0,1:T(8,128)(2,1)S(1)} fusion(bf16[768,2304]{1,0:T(8,128)(2,1)} %bitcast.79, bf16[128,768]{1,0:T(8,128)(2,1)S(1)} %copy-done.13, f32[2304]{0:T(1024)S(1)} %pad_maximum_fusion.3), kind=kOutput, calls=%fused_computation.8 | convolution fusion | flops 453574656 | bytes 4334592 | tf_op jit(solution)/shard_map/dot_general | solution.py:322
  86.2 0.1 fusion.42
  86.3 0.3 fusion.58
  86.7 0.1 exponential_reduce_fusion
  86.8 0.2 convolution_convert_fusion.6
  87.1 0.5 copy-done.1
  87.6 0.4 fusion.59
  88.1 0.2 multiply_reduce_fusion.4
  88.4 0.9 convolution_add_fusion.1
  89.3 1.0 fusion.60
  90.4 0.5 copy-done.32
  90.9 0.2 multiply_reduce_fusion.3
  91.1 0.5 add_rsqrt_fusion
  91.6 1.6 copy.93
  93.2 0.7 convert_reduce_fusion.6
  93.9 1.5 fusion.25
  95.5 0.5 broadcast_multiply_fusion.2
  96.0 0.1 copy.94
  96.1 2.6 %fusion.51 = (bf16[768]{0:T(1024)(128)(2,1)}, f32[128,768]{1,0:T(8,128)S(1)}, bf16[128,768]{1,0:T(8,128)(2,1)}) fusion(f32[128]{0:T(128)} %get-tuple-element.81, f32[128,768]{1,0:T(8,128)S(1)} %get-tuple-element.75, f32[128]{0:T(128)} %copy-done.32, f32[128]{0:T(128)} %get-tuple-element.82, f32[768]{0:T(1024)} %copy-done.17, bf16[128,768]{1,0:T(8,128)(2,1)} %param.33, ...), kind=kLoop, calls=%fused_computation.108 | loop fusion | flops 1178880 | bytes 1189376 | tf_op jit(solution)/shard_map/reduce_sum | solution.py:363
  98.8 4.7 %fusion.63 = (bf16[3072]{0:T(1024)(128)(2,1)}, bf16[128,3072]{1,0:T(8,128)(2,1)S(1)}) fusion(f32[128,3072]{1,0:T(8,128)S(1)} %convolution_add_fusion.1, bf16[3072,768]{1,0:T(8,128)(2,1)} %bitcast.73, f32[128,768]{1,0:T(8,128)S(1)} %get-tuple-element.56), kind=kOutput, calls=%fused_computation.117 | convolution fusion | flops 608400384 | bytes 7477248 | tf_op jit(solution)/shard_map/rd,fd->rf/dot_general | solution.py:365
  103.5 2.3 %multiply_reduce_fusion.1 = (bf16[768]{0:T(1024)(128)(2,1)}, f32[128]{0:T(128)S(1)}, f32[128]{0:T(128)S(1)}, bf16[768]{0:T(1024)(128)(2,1)}, f32[128,768]{1,0:T(8,128)S(1)}) fusion(f32[128,768]{1,0:T(8,128)S(1)} %get-tuple-element.73, f32[128]{0:T(128)S(1)} %copy-done.22, f32[128]{0:T(128)S(1)} %copy-done.19, f32[768]{0:T(1024)S(1)} %get-tuple-element.42, ...), kind=kOutput, calls=%fused_computation.55 | convolution fusion | flops 604961024 | bytes 6692864 | tf_op jit(solution)/shard_map/rf,df->rd/dot_general | solution.py:369
  105.9 0.8 fusion.53
  106.6 0.5 copy-done.2
  107.1 1.2 convolution_convert_fusion.5
  108.4 1.7 copy.82
  110.1 2.6 %fusion.55 = (bf16[12,64]{1,0:T(8,128)(2,1)}, bf16[128,12,64]{0,2,1:T(8,128)(2,1)}) fusion(bf16[128,12,64]{0,2,1:T(8,128)(2,1)} %bitcast.87, f32[12,128,128]{1,2,0:T(8,128)S(1)} %get-tuple-element.71, f32[12,128]{1,0:T(8,128)S(1)} %log_add_fusion), kind=kOutput, calls=%fused_computation.111 | convolution fusion | flops 25754880 | bytes 1187328 | tf_op jit(solution)/shard_map/hqk,qhd->khd/dot_general | solution.py:382
  112.7 2.3 fusion.64
  115.0 2.6 %convolution_convert_fusion.4 = bf16[12,64,128]{2,1,0:T(8,128)(2,1)} fusion(bf16[128,12,64]{0,2,1:T(8,128)(2,1)} %bitcast.97, f32[12,128,128]{1,2,0:T(8,128)} %fusion.64, f32[12,128,128]{1,2,0:T(8,128)S(1)} %get-tuple-element.71, f32[12,128]{1,0:T(8,128)S(1)} %log_add_fusion), kind=kOutput, calls=%fused_computation.31 | convolution fusion | flops 26642048 | bytes 1972224 | tf_op jit(solution)/shard_map/hqk,qhd->khd/dot_general | solution.py:389
  117.6 3.3 %fusion.56 = (bf16[12,64]{1,0:T(8,128)(2,1)}, bf16[128,12,64]{0,2,1:T(8,128)(2,1)}) fusion(bf16[128,12,64]{0,2,1:T(8,128)(2,1)} %bitcast.95, f32[12,128,128]{1,2,0:T(8,128)} %fusion.64, f32[12,128,128]{1,2,0:T(8,128)S(1)} %get-tuple-element.71, f32[12,128]{1,0:T(8,128)S(1)} %log_add_fusion), kind=kOutput, calls=%fused_computation.112 | convolution fusion | flops 26739584 | bytes 1973760 | tf_op jit(solution)/shard_map/hqk,khd->qhd/dot_general | solution.py:386
  120.9 4.4 %convolution_add_fusion.3 = f32[128,768]{1,0:T(8,128)} fusion(f32[128,768]{1,0:T(8,128)S(1)} %get-tuple-element.58, bf16[768,2304]{1,0:T(8,128)(2,1)} %bitcast.80, bf16[128,768]{0,1:T(8,128)(2,1)} %bitcast.81, bf16[128,768]{0,1:T(8,128)(2,1)} %bitcast.90, bf16[128,768]{0,1:T(8,128)(2,1)} %bitcast.92), kind=kOutput, calls=%fused_computation.27 | convolution fusion | flops 454852608 | bytes 4915200 | tf_op jit(solution)/shard_map/re,de->rd/dot_general | solution.py:396
  125.3 2.9 %convolution_convert_fusion.2 = bf16[2304,768]{0,1:T(8,128)(2,1)} fusion(bf16[128,768]{1,0:T(8,128)(2,1)S(1)} %copy-done.14, bf16[128,768]{0,1:T(8,128)(2,1)S(1)} %bitcast.82, bf16[128,768]{0,1:T(8,128)(2,1)S(1)} %bitcast.91, bf16[128,768]{0,1:T(8,128)(2,1)S(1)} %bitcast.93), kind=kOutput, calls=%fused_computation.3 | convolution fusion | flops 456523776 | bytes 4325376 | tf_op jit(solution)/shard_map/ra,rb->ab/dot_general | solution.py:256
  128.2 1.5 convolution_convert_fusion.3
  129.8 3.6 %convolution_convert_fusion.1 = bf16[768,3072]{1,0:T(8,128)(2,1)} fusion(bf16[128,3072]{1,0:T(8,128)(2,1)S(1)} %copy-done.4, f32[128,768]{1,0:T(8,128)S(1)} %get-tuple-element.73, f32[768]{0:T(1024)S(1)} %get-tuple-element.43, f32[768]{0:T(1024)S(1)} %get-tuple-element.42, f32[128]{0:T(128)S(1)} %copy-done.23, f32[128]{0:T(128)S(1)} %copy-done.20), kind=kOutput, calls=%fused_computation.2 | convolution fusion | flops 606830592 | bytes 5905408 | tf_op jit(solution)/shard_map/ra,rb->ab/dot_general | solution.py:256
  133.5 3.6 %convolution_convert_fusion = bf16[3072,768]{1,0:T(8,128)(2,1)} fusion(f32[128,768]{1,0:T(8,128)S(1)} %get-tuple-element.56, f32[128,3072]{1,0:T(8,128)S(1)} %convolution_add_fusion.1), kind=kOutput, calls=%fused_computation.1 | convolution fusion | flops 608403456 | bytes 6684672 | tf_op jit(solution)/shard_map/ra,rb->ab/dot_general | solution.py:256
  137.4 0.4 reshape.280
  137.9 0.1 copy.86
  138.1 0.2 copy.95
  138.3 0.7 pad.10.clone
  139.0 80.7 %scatter_all.1 = (f32[24,2304]{1,0:T(8,128)}, f32[24,768]{1,0:T(8,128)}, f32[24,3072]{1,0:T(8,128)}, f32[96,768]{1,0:T(8,128)}, f32[24,128]{1,0:T(8,128)}) custom-call(bf16[32,24,2304]{2,1,0:T(8,128)(2,1)} %bitcast.71, bf16[32,24,768]{2,1,0:T(8,128)(2,1)} %bitcast.72, bf16[32,24,3072]{2,1,0:T(8,128)(2,1)} %bitcast.61, bf16[32,96,768]{2,1,0:T(8,128)(2,1)} %bitcast.60, ...), custom_call_target="tpu_custom_call" | custom-call | tf_op jit(solution)/shard_map/scatter_all/pallas_call | solution.py:209
  219.7 1.8 slice_reduce_fusion
  221.6 0.8 slice.80
  222.3 0.6 reshape.282
  222.9 1.6 copy.100
  224.6 1.5 copy.101
  226.1 1.7 copy.102
  227.8 1.7 copy.103
  (105 shorter events, 0.7 us)
Async XLA Ops:
  77.7 4.1 %copy-start = (bf16[32,24,128]{2,1,0:T(8,128)(2,1)S(1)}, bf16[32,24,128]{2,1,0:T(8,128)(2,1)}, u32[]{:S(2)}) copy-start(bf16[32,24,128]{2,1,0:T(8,128)(2,1)} %get-tuple-element.26) | copy-start | bytes 589828
  77.7 4.7 %copy-start.13 = (bf16[128,768]{1,0:T(8,128)(2,1)S(1)}, bf16[128,768]{1,0:T(8,128)(2,1)}, u32[]{:S(2)}) copy-start(bf16[128,768]{1,0:T(8,128)(2,1)} %param.17) | copy-start | bytes 589828
  81.8 6.6 %slice-start = ((s8[4718592]{0:T(1024)(128)(4,1)}), s8[4194304]{0:T(1024)(128)(4,1)S(1)}, s32[]{:S(2)}) async-start(s8[4718592]{0:T(1024)(128)(4,1)} %bitcast.62), calls=%async_computation | async-start | bytes 8388608
  82.4 3.8 %copy-start.35 = (s32[128]{0:T(128)S(1)}, s32[128]{0:T(128)}, u32[]{:S(2)}) copy-start(s32[128]{0:T(128)} %param.19) | copy-start | bytes 1540
  82.4 3.8 %copy-start.34 = (s32[128]{0:T(128)S(1)}, s32[128]{0:T(128)}, u32[]{:S(2)}) copy-start(s32[128]{0:T(128)} %param.18) | copy-start | bytes 1540
  82.4 5.9 %slice-start.1 = ((s8[4718592]{0:T(1024)(128)(4,1)}), s8[524288]{0:T(1024)(128)(4,1)S(1)}, s32[]{:S(2)}) async-start(s8[4718592]{0:T(1024)(128)(4,1)} %bitcast.62), calls=%async_computation.1 | async-start | bytes 1048576
  82.4 6.8 %slice-start.4 = ((s8[4718592]{0:T(1024)(128)(4,1)}), s8[4194304]{0:T(1024)(128)(4,1)S(1)}, s32[]{:S(2)}) async-start(s8[4718592]{0:T(1024)(128)(4,1)} %bitcast.74), calls=%async_computation.4 | async-start | bytes 8388608
  86.2 0.7 copy-start.15
  86.2 0.9 copy-start.8
  86.2 0.9 copy-start.16
  86.3 1.3 copy-start.1
  86.8 2.4 %slice-start.5 = ((s8[4718592]{0:T(1024)(128)(4,1)}), s8[524288]{0:T(1024)(128)(4,1)S(1)}, s32[]{:S(2)}) async-start(s8[4718592]{0:T(1024)(128)(4,1)} %bitcast.74), calls=%async_computation.5 | async-start | bytes 1048576
  87.1 1.2 copy-start.6
  88.1 1.1 copy-start.18
  88.4 0.9 copy-start.21
  88.4 0.9 copy-start.24
  89.3 4.6 %copy-start.9 = (bf16[128,768]{1,0:T(8,128)(2,1)S(1)}, bf16[128,768]{1,0:T(8,128)(2,1)}, u32[]{:S(2)}) copy-start(bf16[128,768]{1,0:T(8,128)(2,1)} %param.33) | copy-start | bytes 589828
  90.4 0.5 copy-start.32
  93.9 1.5 copy-start.17
  96.1 7.4 %slice-start.2 = ((s8[4718592]{0:T(1024)(128)(4,1)}), s8[4194304]{0:T(1024)(128)(4,1)S(1)}, s32[]{:S(2)}) async-start(s8[4718592]{0:T(1024)(128)(4,1)} %bitcast.65), calls=%async_computation.2 | async-start | bytes 8388608
  98.8 4.7 %slice-start.3 = ((s8[4718592]{0:T(1024)(128)(4,1)}), s8[524288]{0:T(1024)(128)(4,1)S(1)}, s32[]{:S(2)}) async-start(s8[4718592]{0:T(1024)(128)(4,1)} %bitcast.65), calls=%async_computation.3 | async-start | bytes 1048576
  98.8 4.7 %copy-start.19 = (f32[128]{0:T(128)S(1)}, f32[128]{0:T(128)}, u32[]{:S(2)}) copy-start(f32[128]{0:T(128)} %copy-done.18) | copy-start | bytes 1540
  98.8 4.7 %copy-start.22 = (f32[128]{0:T(128)S(1)}, f32[128]{0:T(128)}, u32[]{:S(2)}) copy-start(f32[128]{0:T(128)} %copy-done.21) | copy-start | bytes 1540
  103.5 2.4 %copy-start.3 = (bf16[128,3072]{1,0:T(8,128)(2,1)}, bf16[128,3072]{1,0:T(8,128)(2,1)S(1)}, u32[]{:S(2)}) copy-start(bf16[128,3072]{1,0:T(8,128)(2,1)S(1)} %get-tuple-element.80) | copy-start | bytes 2359300
  105.9 1.3 copy-start.2
  120.9 4.4 %copy-start.5 = (bf16[128,12,64]{0,2,1:T(8,128)(2,1)S(1)}, bf16[128,12,64]{0,2,1:T(8,128)(2,1)}, u32[]{:S(2)}) copy-start(bf16[128,12,64]{0,2,1:T(8,128)(2,1)} %get-tuple-element.64) | copy-start | bytes 589828
  120.9 4.4 %copy-start.11 = (bf16[12,64,128]{2,1,0:T(8,128)(2,1)S(1)}, bf16[12,64,128]{2,1,0:T(8,128)(2,1)}, u32[]{:S(2)}) copy-start(bf16[12,64,128]{2,1,0:T(8,128)(2,1)} %convolution_convert_fusion.4) | copy-start | bytes 589828
  120.9 4.4 %copy-start.12 = (bf16[128,12,64]{0,2,1:T(8,128)(2,1)S(1)}, bf16[128,12,64]{0,2,1:T(8,128)(2,1)}, u32[]{:S(2)}) copy-start(bf16[128,12,64]{0,2,1:T(8,128)(2,1)} %get-tuple-element.66) | copy-start | bytes 589828
  120.9 4.4 %copy-start.14 = (bf16[128,768]{1,0:T(8,128)(2,1)S(1)}, bf16[128,768]{1,0:T(8,128)(2,1)}, u32[]{:S(2)}) copy-start(bf16[128,768]{1,0:T(8,128)(2,1)} %param.17) | copy-start | bytes 589828
  125.3 2.9 %copy-start.7 = (bf16[12,64,128]{2,1,0:T(8,128)(2,1)S(1)}, bf16[12,64,128]{2,1,0:T(8,128)(2,1)}, u32[]{:S(2)}) copy-start(bf16[12,64,128]{2,1,0:T(8,128)(2,1)} %copy-done.6) | copy-start | bytes 589828
  128.2 1.5 copy-start.4
  128.2 1.5 copy-start.20
  128.2 1.5 copy-start.23
  133.4 3.7 %copy-start.33 = (bf16[12,64]{1,0:T(8,128)(2,1)S(1)}, bf16[12,64]{1,0:T(8,128)(2,1)}, u32[]{:S(2)}) copy-start(bf16[12,64]{1,0:T(8,128)(2,1)} %get-tuple-element.65) | copy-start | bytes 4612
  133.4 3.8 %copy-start.25 = (bf16[12,64]{1,0:T(8,128)(2,1)S(1)}, bf16[12,64]{1,0:T(8,128)(2,1)}, u32[]{:S(2)}) copy-start(bf16[12,64]{1,0:T(8,128)(2,1)} %get-tuple-element.63) | copy-start | bytes 4612
  133.4 3.9 %copy-start.30 = (bf16[768]{0:T(1024)(128)(2,1)S(1)}, bf16[768]{0:T(1024)(128)(2,1)}, u32[]{:S(2)}) copy-start(bf16[768]{0:T(1024)(128)(2,1)} %get-tuple-element.57) | copy-start | bytes 4612
  133.4 3.9 %copy-start.29 = (bf16[768]{0:T(1024)(128)(2,1)S(1)}, bf16[768]{0:T(1024)(128)(2,1)}, u32[]{:S(2)}) copy-start(bf16[768]{0:T(1024)(128)(2,1)} %get-tuple-element.35) | copy-start | bytes 4612
  133.4 3.9 %copy-start.28 = (bf16[768]{0:T(1024)(128)(2,1)S(1)}, bf16[768]{0:T(1024)(128)(2,1)}, u32[]{:S(2)}) copy-start(bf16[768]{0:T(1024)(128)(2,1)} %get-tuple-element.40) | copy-start | bytes 4612
  133.4 3.9 %copy-start.27 = (bf16[768]{0:T(1024)(128)(2,1)S(1)}, bf16[768]{0:T(1024)(128)(2,1)}, u32[]{:S(2)}) copy-start(bf16[768]{0:T(1024)(128)(2,1)} %get-tuple-element.55) | copy-start | bytes 4612
  133.4 3.9 %copy-start.26 = (bf16[768]{0:T(1024)(128)(2,1)S(1)}, bf16[768]{0:T(1024)(128)(2,1)}, u32[]{:S(2)}) copy-start(bf16[768]{0:T(1024)(128)(2,1)} %get-tuple-element.37) | copy-start | bytes 4612
  133.4 3.9 %copy-start.10 = (bf16[128,768]{1,0:T(8,128)(2,1)S(1)}, bf16[128,768]{1,0:T(8,128)(2,1)}, u32[]{:S(2)}) copy-start(bf16[128,768]{1,0:T(8,128)(2,1)} %param.33) | copy-start | bytes 589828
  133.5 4.0 %copy-start.31 = (bf16[3072]{0:T(1024)(128)(2,1)S(1)}, bf16[3072]{0:T(1024)(128)(2,1)}, u32[]{:S(2)}) copy-start(bf16[3072]{0:T(1024)(128)(2,1)} %get-tuple-element.79) | copy-start | bytes 18436

commit v2 on v1

--- a/solution.py
+++ b/solution.py
@@ -15,9 +15,9 @@
 GROUP = 32
 CORE, X, Y, Z1, Z2 = 0, 1, 2, 3, 4
 SCATTER_ORDERS = (
-    (CORE, X, Y, Z2, Z1),
-    (CORE, X, Y, Z2, Z1),
-    (CORE, Y, X, Z2, Z1),
+    (CORE, X, Y, Z1, Z2),
+    (CORE, X, Y, Z1, Z2),
+    (CORE, Y, X, Z1, Z2),
     (CORE, Z1, Z2, X, Y),
     (CORE, Z1, Z2, X, Y),
 )
@@ -252,6 +252,73 @@
     return jnp.where(visible[None], scores, -1e30)
 
 
+def vector_rows(vectors):
+    rows = [jnp.pad(v, ((0, 0), (0, 128 - v.shape[1]))) for v in vectors]
+    rows = rows + [jnp.zeros_like(rows[0])] * (16 - len(rows))
+    return jnp.stack(rows, axis=1)
+
+
+def attention_back_kernel(
+    scale, qkv_ref, back_ref, doc_col, doc_row, pad_row, d_qkv_ref, sums_ref
+):
+    fl = jnp.float32
+    rows, width = back_ref.shape
+    size = width // HEADS
+    across, down, both = ((1,), (0,)), ((0,), (0,)), ((1,), (1,))
+
+    def dot(a, b, over):
+        return lax.dot_general(a, b, (over, ((), ())), preferred_element_type=fl)
+
+    square = (rows, rows)
+    same = lax.broadcasted_iota(jnp.int32, square, 0) == lax.broadcasted_iota(
+        jnp.int32, square, 1
+    )
+    visible = (doc_col[...] == doc_row[...]) & ((pad_row[...] == 1) | same)
+    for pair in range(HEADS // 2):
+        results = []
+        for h in (2 * pair, 2 * pair + 1):
+            query, key_rows, value_rows = (
+                qkv_ref[:, part * width + h * size : part * width + (h + 1) * size]
+                for part in range(3)
+            )
+            back = back_ref[:, h * size : (h + 1) * size]
+            scores = jnp.where(visible, dot(query, key_rows, both) * scale, -1e30)
+            row_max = jnp.max(scores, axis=-1, keepdims=True)
+            total = jnp.sum(jnp.exp(scores - row_max), axis=-1, keepdims=True)
+            probs = jnp.exp(scores - (row_max + jnp.log(total)))
+            d_value = dot(probs.astype(jnp.bfloat16), back, down)
+            d_probs = dot(back, value_rows, both)
+            delta = jnp.sum(probs * d_probs, axis=-1, keepdims=True)
+            d_scores = (probs * (d_probs - delta) * scale).astype(jnp.bfloat16)
+            results.append(
+                (dot(d_scores, key_rows, across), dot(d_scores, query, down), d_value)
+            )
+        for part in range(3):
+            block = jnp.concatenate([results[0][part], results[1][part]], axis=1)
+            at = pair * 2 * size
+            d_qkv_ref[:, part * width + at : part * width + at + 2 * size] = block.astype(
+                jnp.bfloat16
+            )
+            if part != 1:
+                row = part // 2
+                sums_ref[row : row + 1, at : at + 2 * size] = jnp.sum(
+                    block, axis=0, keepdims=True
+                )
+
+
+def attention_back(qkv, d_context, doc_ids, pad_mask):
+    rows, width = d_context.shape
+    return pl.pallas_call(
+        functools.partial(attention_back_kernel, 1.0 / math.sqrt(width // HEADS)),
+        out_shape=(
+            jax.ShapeDtypeStruct(qkv.shape, jnp.bfloat16),
+            jax.ShapeDtypeStruct((2, width), jnp.float32),
+        ),
+        compiler_params=pltpu.CompilerParams(vmem_limit_bytes=24 * 1024 * 1024),
+        name="attention_back",
+    )(qkv, d_context, doc_ids[:, None], doc_ids[None], pad_mask[None])
+
+
 def grad_rows(left, right):
     return jnp.einsum("ra,rb->ab", left, right, preferred_element_type=jnp.float32)
 
@@ -277,28 +344,19 @@
 ):
     fl = jnp.float32
     in_kernels = lax.axis_size(AXIS) == GROUP
-    vectors = jnp.concatenate(
-        [
-            jnp.stack(
-                [
-                    query_bias,
-                    value_bias,
-                    out_bias,
-                    attn_gain,
-                    attn_shift,
-                    down_bias,
-                    ffn_gain,
-                    ffn_shift,
-                ],
-                axis=1,
-            ),
-            up_bias.reshape(query_bias.shape[0], -1),
-        ],
-        axis=1,
-    )
-    vector_count = vectors.shape[1]
+    owned_vectors = (
+        query_bias,
+        value_bias,
+        out_bias,
+        attn_gain,
+        attn_shift,
+        down_bias,
+        ffn_gain,
+        ffn_shift,
+        up_bias,
+    )
+    vectors = vector_rows([v[None] for v in owned_vectors])[0]
     if in_kernels:
-        vectors = jnp.pad(vectors, ((0, 0), (0, 128 - vector_count)))
         wholes = gather_all([qkv_matrix, out_matrix, up_matrix, down_matrix, vectors])
         wholes = [w.reshape((-1, w.shape[-1])) for w in wholes]
     else:
@@ -307,10 +365,18 @@
             for w in (qkv_matrix, out_matrix, up_matrix, down_matrix, vectors)
         ]
     qkv_full, outm_full, upm_full, downm_full, vectors_full = wholes
-    qbias_full, vbias_full, outb_full, gain_one, shift_one, downb_full, gain_two, shift_two = (
-        vectors_full[:, j] for j in range(8)
-    )
-    upb_full = vectors_full[:, 8:vector_count].reshape(-1)
+    vectors_full = vectors_full.reshape((-1,) + vectors.shape)
+    (
+        qbias_full,
+        vbias_full,
+        outb_full,
+        gain_one,
+        shift_one,
+        downb_full,
+        gain_two,
+        shift_two,
+        upb_full,
+    ) = (vectors_full[:, j, : v.shape[0]].reshape(-1) for j, v in enumerate(owned_vectors))
     qkv_back, outm_back, upm_back, downm_back = qkv_full, outm_full, upm_full, downm_full
     gain_one_back, gain_two_back = gain_one, gain_two
     row_count, model_width = tokens.shape
@@ -375,72 +441,54 @@
     d_context = jnp.einsum("re,de->rd", d_attn_b, outm_back, preferred_element_type=fl).astype(
         jnp.bfloat16
     )
-    d_context = d_context.reshape(row_count, HEADS, head_size)
-    again_scores = masked_scores(query, key_rows, visible, score_scale)
-    probs_f = jnp.exp(again_scores - log_total)
-    again_probs = probs_f.astype(jnp.bfloat16)
-    d_value = jnp.einsum("hqk,qhd->khd", again_probs, d_context, preferred_element_type=fl)
-    d_probs = jnp.einsum("qhd,khd->hqk", d_context, value_rows, preferred_element_type=fl)
-    delta = jnp.sum(probs_f * d_probs, axis=-1, keepdims=True)
-    d_scores = (probs_f * (d_probs - delta) * score_scale).astype(jnp.bfloat16)
-    d_query = jnp.einsum("hqk,khd->qhd", d_scores, key_rows, preferred_element_type=fl).reshape(
-        row_count, model_width
-    )
-    d_key = jnp.einsum("hqk,qhd->khd", d_scores, query, preferred_element_type=fl).reshape(
-        row_count, model_width
-    )
-    d_value = d_value.reshape(row_count, model_width)
-    g_qbias = jnp.sum(d_query, axis=0)
-    g_vbias = jnp.sum(d_value, axis=0)
-    d_qkv = jnp.concatenate([d_query, d_key, d_value], axis=1).astype(jnp.bfloat16)
+    d_qkv, attn_sums = attention_back(qkv, d_context, doc_ids, pad_mask)
+    g_qbias, g_vbias = attn_sums[0], attn_sums[1]
     token_grad = d_attn + jnp.einsum("re,de->rd", d_qkv, qkv_back, preferred_element_type=fl)
-    sums = jnp.concatenate(
+    sums = vector_rows(
         [
-            jnp.stack(
-                [
-                    g_qbias,
-                    g_vbias,
-                    g_out_b,
-                    g_gain_one,
-                    g_shift_one,
-                    g_down_b,
-                    g_gain_two,
-                    g_shift_two,
-                ],
-                axis=1,
-            ),
-            g_up_b.reshape(model_width, ratio),
-        ],
-        axis=1,
+            g.reshape((lax.axis_size(AXIS), -1))
+            for g in (
+                g_qbias,
+                g_vbias,
+                g_out_b,
+                g_gain_one,
+                g_shift_one,
+                g_down_b,
+                g_gain_two,
+                g_shift_two,
+                g_up_b,
+            )
+        ]
     )
     pairs = ((tokens, d_qkv), (context, d_attn_b), (hidden_b, d_pre_b), (activation, d_ffn_b))
     if in_kernels:
         parts = [grad_rows(left, right).astype(jnp.bfloat16) for left, right in pairs]
-        parts.append(jnp.pad(sums, ((0, 0), (0, 128 - vector_count))).astype(jnp.bfloat16))
-        owned = scatter_all([p.reshape((GROUP, -1, p.shape[1])) for p in parts])
+        parts = [p.reshape((GROUP, -1, p.shape[1])) for p in parts]
+        owned = scatter_all(parts + [sums.astype(jnp.bfloat16)])
     else:
         owned = [
             lax.psum_scatter(p, AXIS, scatter_dimension=0, tiled=True)
-            for p in [grad_rows(left, right) for left, right in pairs] + [sums]
+            for p in [grad_rows(left, right) for left, right in pairs]
+            + [sums.reshape((-1, sums.shape[2]))]
         ]
     grad_qkv, grad_outmat, grad_upmat, grad_downmat, vec = owned
-    grad_upbias = vec[:, 8:vector_count].reshape(-1)
+    owned_sums = [vec[j, : v.shape[0]] for j, v in enumerate(owned_vectors)]
     return (
         layer_out,
         token_grad,
         grad_qkv,
-        vec[:, 0],
-        vec[:, 1],
+        owned_sums[0],
+        owned_sums[1],
         grad_outmat,
-        vec[:, 2],
-        vec[:, 3],
-        vec[:, 4],
+        owned_sums[2],
+        owned_sums[3],
+        owned_sums[4],
         grad_upmat,
-        grad_upbias,
+        owned_sums[8],
         grad_downmat,
-        vec[:, 5],
-        vec[:, 6],
-        vec[:, 7],
+        owned_sums[5],
+        owned_sums[6],
+        owned_sums[7],
     )
 
 

time: 230 us -> 206 us (0.90)
  matrix products: 41.7 us -> 33.1 us
  local copies, waits for them, and re-layouts: 26.6 us -> 19.5 us
  other arithmetic: 9.61 us -> 4.85 us
  Pallas kernels: 150 us -> 146 us
    dot_general x4 -> x0, matrix products: 10.8 us -> none  [the longest x1 3.34 us: local(): jnp.einsum('hqk,khd->qhd', d_scores, key_rows, preferred_element_type=fl)]
    pallas_call x1, Pallas kernels: 80.7 us -> 72 us  [scatter_all(): pl.pallas_call(functools.partial(scatter_kernel, count), out_shape=[jax.S...]
    pallas_call x0 -> x1, Pallas kernels: none -> 5.81 us  [attention_back(): pl.pallas_call(functools.partial(attention_back_kernel, 1.0 / math.sqrt(w...]
    slice x3, local copies, waits for them, and re-layouts: 4.66 us -> 0.36 us  [the longest x1 0.17 us: local(): query = qkv[:, :model_width].reshape(row_count, HEADS, head_size)]
    squeeze x0 -> x2, local copies, waits for them, and re-layouts: none -> 2.71 us  [local(): owned_sums = [vec[j, :v.shape[0]] for j, v in enumerate(owned_vectors)]]
    dot_general x1, matrix products: 1.04 us -> 3.42 us  [local(): jnp.dot(activation, downm_full, preferred_element_type=fl)]
    dot_general x1, matrix products: 0.86 us -> 3.2 us  [local(): jnp.dot(hidden_b, upm_full, preferred_element_type=fl) + upb_full.astype(fl)]
    unnamed x92 -> x34, local copies, waits for them, and re-layouts: 10.3 us -> 8.25 us
where the time goes in v2:
time: 206 us; the launch traced here: 205 us
  Pallas kernels  146 us (71%)
  matrix products  33.1 us (16%)
  local copies, waits for them, and re-layouts  19.5 us (9%)
  other arithmetic  4.85 us (2%)
    pallas_call x1, Pallas kernels, scatter_all(): pl.pallas_call(functools.partial(scatter_kernel, count), out_shape=[jax.S...  72 us
    pallas_call x1, Pallas kernels, gather_all(): pl.pallas_call(functools.partial(gather_kernel, count), out_shape=[jax.Sh...  68.5 us
    dot_general x4, matrix products, grad_rows(): jnp.einsum('ra,rb->ab', left, right, preferred_element_type=jnp.float32)  11.7 us
    unnamed x34, local copies, waits for them, and re-layouts  8.25 us
    another operation x31, local copies, waits for them, and re-layouts, vector_rows(): return jnp.stack(rows, axis=1)  6.36 us
    pallas_call x1, Pallas kernels, attention_back(): pl.pallas_call(functools.partial(attention_back_kernel, 1.0 / math.sqrt(w...  5.81 us
    dot_general x1, matrix products, local(): jnp.einsum('rd,fd->rf', d_ffn_b, downm_back, preferred_element_type=fl)  4.67 us

profile of v2, /device:TPU:0, one launch (start us, length us, event | category | flops | bytes accessed | tf_op | source)
XLA Modules:
  0.0 205.1 jit_solution(12661040819680767405)
XLA Ops:
  0.6 0.7 pad_bitcast_fusion.17
  1.3 0.7 pad_bitcast_fusion.15
  2.0 0.7 pad_bitcast_fusion.13
  2.7 0.7 pad_bitcast_fusion.11
  3.3 0.7 pad_bitcast_fusion.9
  4.0 1.2 stack.93
  5.2 68.5 %gather_all.1 = (bf16[32,24,2304]{2,1,0:T(8,128)(2,1)}, bf16[32,24,768]{2,1,0:T(8,128)(2,1)}, bf16[32,24,3072]{2,1,0:T(8,128)(2,1)}, bf16[32,96,768]{2,1,0:T(8,128)(2,1)}, bf16[32,16,128]{2,1,0:T(8,128)(2,1)}) custom-call(bf16[24,2304]{1,0:T(8,128)(2,1)} %refs_0_.1, bf16[24,768]{1,0:T(8,128)(2,1)} %refs_1_.1, bf16[24,3072]{1,0:T(8,128)(2,1)} %refs_2_.1, ...), custom_call_target="tpu_custom_call" | custom-call | tf_op jit(solution)/shard_map/gather_all/pallas_call | solution.py:113
  73.8 1.9 convert_reduce_fusion.1
  75.7 0.1 reshape.278
  75.8 0.9 convert_reduce_fusion.3
  76.7 0.1 reshape.277
  76.8 0.1 reshape.274
  76.9 0.1 reshape.273
  76.9 0.1 reshape.272
  77.1 2.8 %fusion.1.qkv_ref = bf16[128,2304]{1,0:T(8,128)(2,1)S(1)} fusion(bf16[128,768]{1,0:T(8,128)(2,1)} %param.17, bf16[768,2304]{1,0:T(8,128)(2,1)} %bitcast.114, f32[2304]{0:T(1024)S(1)} %pad_maximum_fusion), kind=kOutput, calls=%fused_computation.7 | convolution fusion | flops 453574656 | bytes 4334592 | tf_op jit(solution)/shard_map/dot_general | solution.py:388
  79.9 0.2 copy.39
  80.1 0.2 copy.40
  80.2 0.2 copy.41
  80.4 0.1 copy-done.1
  80.5 0.1 fusion.25
  80.6 0.3 fusion.32
  81.0 0.1 exponential_reduce_fusion
  81.1 0.2 convolution_convert_fusion.5
  81.4 0.5 copy-done.2
  81.9 0.4 fusion.33
  82.3 0.1 reshape.276
  82.4 0.1 reshape.275
  82.5 0.2 multiply_reduce_fusion.3
  82.7 3.2 %convolution_add_fusion.1 = f32[128,3072]{1,0:T(8,128)S(1)} fusion(bf16[768,3072]{1,0:T(8,128)(2,1)} %bitcast.110, f32[3072]{0:T(1024)S(1)} %reshape.277, f32[128,768]{1,0:T(8,128)S(1)} %get-tuple-element.75, f32[768]{0:T(1024)S(1)} %reshape.276, f32[768]{0:T(1024)S(1)} %reshape.275, f32[128]{0:T(128)S(1)} %add_rsqrt_fusion.1, ...), kind=kOutput, calls=%fused_computation.5 | convolution fusion | flops 604864512 | bytes 6704128 | tf_op jit(solution)/shard_map/dot_general | solution.py:414
  86.0 3.4 %fusion.34 = (f32[128]{0:T(128)S(1)}, f32[128,768]{1,0:T(8,128)S(1)}) fusion(f32[768]{0:T(1024)S(1)} %reshape.278, bf16[3072,768]{1,0:T(8,128)(2,1)} %bitcast.117, f32[128,3072]{1,0:T(8,128)S(1)} %convolution_add_fusion.1, f32[768]{0:T(1024)S(1)} %reshape.276, f32[768]{0:T(1024)S(1)} %reshape.275, f32[128]{0:T(128)S(1)} %add_rsqrt_fusion.1, ...), kind=kOutput, calls=%fused_computation.112 | convolution fusion | flops 606633856 | bytes 7088640 | tf_op jit(solution)/shard_map/dot_general | solution.py:419
  89.4 0.2 multiply_reduce_fusion.2
  89.6 0.1 reshape.279
  89.7 0.3 fusion.15
  90.0 0.1 reshape.280
  90.1 0.9 fusion.28
  91.0 4.7 %fusion.35 = (bf16[3072]{0:T(1024)(128)(2,1)S(1)}, bf16[128,3072]{1,0:T(8,128)(2,1)S(1)}) fusion(f32[128,3072]{1,0:T(8,128)S(1)} %convolution_add_fusion.1, bf16[3072,768]{1,0:T(8,128)(2,1)} %bitcast.118, f32[128,768]{1,0:T(8,128)S(1)} %get-tuple-element.57), kind=kOutput, calls=%fused_computation.113 | convolution fusion | flops 608400384 | bytes 7477248 | tf_op jit(solution)/shard_map/rd,fd->rf/dot_general | solution.py:431
  95.7 1.8 multiply_reduce_fusion
  97.5 0.2 fusion.30
  97.7 1.1 copy-done.3
  98.8 0.5 convolution_convert_fusion.4.back_ref
  99.3 0.1 copy.43.doc_col
  99.4 5.8 %attention_back.1 = (bf16[128,2304]{1,0:T(8,128)(2,1)S(1)}, f32[2,768]{1,0:T(2,128)S(1)}) custom-call(bf16[128,2304]{1,0:T(8,128)(2,1)S(1)} %fusion.1.qkv_ref, bf16[128,768]{1,0:T(8,128)(2,1)S(1)} %convolution_convert_fusion.4.back_ref, s32[128,1]{1,0:T(8,128)S(1)} %copy.43.doc_col, s32[1,128]{1,0:T(1,128)S(1)} %bitcast.105, s32[1,128]{1,0:T(1,128)S(1)} %bitcast.106), custom_call_target="tpu_custom_call" | custom-call | tf_op jit(solution)/shard_map/attention_back/pallas_call | solution.py:311
  105.3 4.0 %convolution_add_fusion.3 = f32[128,768]{1,0:T(8,128)} fusion(f32[128,768]{1,0:T(8,128)S(1)} %get-tuple-element.59, bf16[128,2304]{1,0:T(8,128)(2,1)S(1)} %get-tuple-element.32, bf16[768,2304]{1,0:T(8,128)(2,1)} %bitcast.115), kind=kOutput, calls=%fused_computation.20 | convolution fusion | flops 453083136 | bytes 4915200 | tf_op jit(solution)/shard_map/re,de->rd/dot_general | solution.py:446
  109.3 2.9 %convolution_convert_fusion.2 = bf16[2304,768]{0,1:T(8,128)(2,1)} fusion(bf16[128,2304]{1,0:T(8,128)(2,1)S(1)} %get-tuple-element.32, bf16[128,768]{1,0:T(8,128)(2,1)S(1)} %copy-done.8), kind=kOutput, calls=%fused_computation.2 | convolution fusion | flops 454754304 | bytes 4325376 | tf_op jit(solution)/shard_map/ra,rb->ab/dot_general | solution.py:323
  112.2 1.5 convolution_convert_fusion.3
  113.7 3.6 %convolution_convert_fusion.1 = bf16[768,3072]{1,0:T(8,128)(2,1)} fusion(bf16[128,3072]{1,0:T(8,128)(2,1)S(1)} %copy-done.7, f32[128,768]{1,0:T(8,128)S(1)} %get-tuple-element.75, f32[768]{0:T(1024)S(1)} %reshape.276, f32[768]{0:T(1024)S(1)} %reshape.275, f32[128]{0:T(128)S(1)} %add_rsqrt_fusion.1, f32[128]{0:T(128)S(1)} %broadcast_multiply_fusion.5), kind=kOutput, calls=%fused_computation.1 | convolution fusion | flops 606830592 | bytes 5905408 | tf_op jit(solution)/shard_map/ra,rb->ab/dot_general | solution.py:323
  117.3 3.6 %convolution_convert_fusion = bf16[3072,768]{1,0:T(8,128)(2,1)} fusion(f32[128,768]{1,0:T(8,128)S(1)} %copy-done.5, f32[128,3072]{1,0:T(8,128)S(1)} %convolution_add_fusion.1), kind=kOutput, calls=%fused_computation | convolution fusion | flops 608403456 | bytes 6684672 | tf_op jit(solution)/shard_map/ra,rb->ab/dot_general | solution.py:323
  121.0 0.1 reshape_squeeze.6
  121.1 0.1 reshape_squeeze.7
  121.3 0.1 reshape.265
  121.4 0.1 reshape.266
  121.5 0.1 reshape.267
  121.7 0.1 reshape.268
  121.8 0.1 reshape.269
  122.0 0.1 reshape.270
  122.1 0.1 reshape.271
  122.3 1.5 stack.105.refs_4_
  123.8 72.0 %scatter_all.1 = (f32[24,2304]{1,0:T(8,128)}, f32[24,768]{1,0:T(8,128)}, f32[24,3072]{1,0:T(8,128)}, f32[96,768]{1,0:T(8,128)}, f32[16,128]{1,0:T(8,128)}) custom-call(bf16[32,24,2304]{2,1,0:T(8,128)(2,1)} %bitcast.109, bf16[32,24,768]{2,1,0:T(8,128)(2,1)} %bitcast.116, bf16[32,24,3072]{2,1,0:T(8,128)(2,1)} %bitcast.108, bf16[32,96,768]{2,1,0:T(8,128)(2,1)} %bitcast.107, ...), custom_call_target="tpu_custom_call" | custom-call | tf_op jit(solution)/shard_map/scatter_all/pallas_call | solution.py:209
  195.9 1.5 slice_bitcast_fusion
  197.4 1.2 slice_bitcast_fusion.3
  198.6 1.6 copy.59
  200.2 1.5 copy.60
  201.7 1.7 copy.61
  203.4 1.7 copy.62
  (68 shorter events, 0.5 us)
Async XLA Ops:
  79.8 0.7 copy-start.1
  79.8 0.7 copy-start
  80.6 1.3 copy-start.2
  80.6 1.3 copy-start.8
  81.4 1.4 copy-start.9
  85.9 3.7 %copy-start.11 = (bf16[128,768]{1,0:T(8,128)(2,1)S(1)}, bf16[128,768]{1,0:T(8,128)(2,1)}, u32[]{:S(2)}) copy-start(bf16[128,768]{1,0:T(8,128)(2,1)} %param.33) | copy-start | bytes 589828
  90.1 5.6 %slice-start = ((s8[4718592]{0:T(1024)(128)(4,1)}), s8[4194304]{0:T(1024)(128)(4,1)S(1)}, s32[]{:S(2)}) async-start(s8[4718592]{0:T(1024)(128)(4,1)} %bitcast.111), calls=%async_computation | async-start | bytes 8388608
  91.0 4.7 %copy-start.4 = (f32[128,768]{1,0:T(8,128)}, f32[128,768]{1,0:T(8,128)S(1)}, u32[]{:S(2)}) copy-start(f32[128,768]{1,0:T(8,128)S(1)} %get-tuple-element.57) | copy-start | bytes 1179652
  91.0 4.7 %slice-start.1 = ((s8[4718592]{0:T(1024)(128)(4,1)}), s8[524288]{0:T(1024)(128)(4,1)S(1)}, s32[]{:S(2)}) async-start(s8[4718592]{0:T(1024)(128)(4,1)} %bitcast.111), calls=%async_computation.1 | async-start | bytes 1048576
  95.6 1.9 copy-start.6
  97.5 1.3 copy-start.3
  109.3 2.9 %copy-start.10 = (bf16[12,64,128]{2,1,0:T(8,128)(2,1)S(1)}, bf16[12,64,128]{2,1,0:T(8,128)(2,1)}, u32[]{:S(2)}) copy-start(bf16[12,64,128]{2,1,0:T(8,128)(2,1)} %copy-done.9) | copy-start | bytes 589828
  112.2 1.5 copy-start.7
  113.7 3.6 %copy-start.5 = (f32[128,768]{1,0:T(8,128)S(1)}, f32[128,768]{1,0:T(8,128)}, u32[]{:S(2)}) copy-start(f32[128,768]{1,0:T(8,128)} %copy-done.4) | copy-start | bytes 1179652
  117.3 4.6 %copy-start.12 = (bf16[128,768]{1,0:T(8,128)(2,1)S(1)}, bf16[128,768]{1,0:T(8,128)(2,1)}, u32[]{:S(2)}) copy-start(bf16[128,768]{1,0:T(8,128)(2,1)} %param.33) | copy-start | bytes 589828
